TPU v7x, 512 devices: a whole 4x8x8 slice. The times are simulated.
512 devices in a mesh: corpus: 64 (over y, x, core), tile: 8 (over z).
Axes of the slice: x: 4, y: 8, z: 8, core: 2. Of those that a mesh axis runs over, the one named last changes fastest.
Arguments:
- embeddings: bfloat16 [131072, 1024], P('corpus'), may hold values from -250 to 250
- cluster_ids: int32 [131072], P('corpus'), may hold values from 0 to 63, as said below
Outputs:
- best_match: float32 [131072], P('corpus')
Inputs may be any that keep to these rules, and one draw needn't show every extreme that they name: `cluster_ids`: within each aligned block of 2048 rows (the rows of one index of corpus) no cluster appears more than 64 times, and one cluster appears exactly 64 times in every block.
All inputs are finite; a program needn't handle non-finite values.
Results may differ from a plain program's by a relative error of at most 0.00055.
Values may be sent and summed in bfloat16 or wider, within the bound.
A program may use at most 64 MiB of HBM per device.

v0:
```python
import jax
import jax.numpy as jnp
from jax import lax
from jax.sharding import PartitionSpec as P

EPS = 1e-06


def unit_rows(embeddings):
    values = embeddings.astype(jnp.float32)
    total = jnp.sum(values * values, axis=-1, keepdims=True)
    return (values * lax.rsqrt(total + EPS)).astype(jnp.bfloat16)


def inner(left, right):
    return lax.dot_general(
        left, right, (((1,), (1,)), ((), ())), preferred_element_type=jnp.float32
    )


def local(embeddings, cluster_ids):
    rows_dev = embeddings.shape[0]
    width = embeddings.shape[1]
    corpus = lax.axis_size("corpus")
    tiles = lax.axis_size("tile")
    per_owner = 2 * rows_dev // corpus
    total = corpus * per_owner
    tile_index = lax.axis_index("tile")
    unit = unit_rows(embeddings)
    onehot = (cluster_ids[:, None] == jnp.arange(corpus, dtype=jnp.int32)[None, :]).astype(
        jnp.int32
    )
    before = jnp.cumsum(onehot, axis=0) - onehot
    rank = jnp.sum(before * onehot, axis=1)
    slot = cluster_ids * per_owner + rank
    outbox = (
        jnp.zeros((total, width), jnp.bfloat16).at[slot].set(unit).reshape(corpus, per_owner, width)
    )
    filled = jnp.zeros((total,), jnp.bfloat16).at[slot].set(1.0).reshape(corpus, per_owner)
    inbox, inflag = (
        lax.all_to_all(outbox, "corpus", split_axis=0, concat_axis=0, tiled=True),
        lax.all_to_all(filled, "corpus", split_axis=0, concat_axis=0, tiled=True),
    )
    queries = inbox.reshape(total, width)
    span = total // tiles
    keys = lax.dynamic_slice_in_dim(queries, tile_index * span, span, 0)
    key_ok = lax.dynamic_slice_in_dim(inflag.reshape(total), tile_index * span, span, 0) > 0
    scores = inner(queries, keys)
    query_pos = jnp.arange(total, dtype=jnp.int32)[:, None]
    key_pos = tile_index * span + jnp.arange(span, dtype=jnp.int32)[None, :]
    keep = key_ok[None, :] & (query_pos != key_pos)
    partial_value = jnp.max(jnp.where(keep, scores, jnp.float32(-1.0)), axis=1).reshape(
        corpus, per_owner
    )
    partial_value = lax.pmax(partial_value, "tile")
    returned = lax.all_to_all(partial_value, "corpus", split_axis=0, concat_axis=0, tiled=True)
    best = returned.reshape(total)[slot]
    return best


def solution(mesh):
    in_specs = (P("corpus", None), P("corpus"))
    out_specs = P("corpus")
    return jax.shard_map(local, mesh=mesh, in_specs=in_specs, out_specs=out_specs, check_vma=False)
```

profile of v0, /device:TPU:1, one launch (start us, length us, event | category | flops | bytes accessed | tf_op | source)
XLA Modules:
  0.0 346.3 jit_solution(14538305168302031933)
XLA Ops:
  0.0 0.7 fusion.11
  0.7 18.1 %reduce-window.6 = s32[64,16,128]{2,1,0:T(8,128)S(1)} reduce-window(s32[64,16,128]{2,1,0:T(8,128)S(1)} %fusion.11, s32[]{:T(128)} %constant.13.clone.1), window={size=1x1x128 pad=0_0x0_0x127_0}, to_apply=%region_0.0 | reduce-window | flops 16646144 | bytes 1048580 | tf_op jit(solution)/shard_map/reduce-window
  18.9 0.2 slice.10
  19.1 0.4 copy.8
  19.5 0.2 reduce-window.9
  19.7 0.2 broadcast_add_fusion
  19.9 1.0 fusion.10
  21.0 0.7 broadcast_clamp_fusion
  21.7 14.6 %scatter_custom_fusion = bf16[4096]{0:T(1024)(128)(2,1)S(1)} fusion(s32[2048]{0:T(1024)S(1)} %get-tuple-element.6, bf16[2048]{0:T(1024)(128)(2,1)S(1)} %broadcast.36, bf16[]{:T(256)} %constant.11.clone.1), kind=kCustom, calls=%fused_computation.25 | custom fusion | bytes 8194 | tf_op jit(solution)/shard_map/scatter | solution.py:39
  36.3 0.7 all_to_all.20
  36.9 11.6 %all-to-all-start = ((bf16[64,1,64]{2,1,0:T(2,128)(2,1)}), bf16[64,1,64]{2,1,0:T(2,128)(2,1)S(1)}, u32[]{:S(2)}, u32[]{:S(2)}) async-start(bf16[64,1,64]{2,1,0:T(2,128)(2,1)} %all_to_all.20), calls=%async_computation | async-start | bytes 65536 | tf_op jit(solution)/shard_map/all_to_all | solution.py:42
  48.6 3.1 fusion
  51.7 15.8 %scatter_custom_fusion.1 = bf16[4096,1024]{1,0:T(8,128)(2,1)} fusion(s32[2048]{0:T(1024)S(1)} %get-tuple-element.6, bf16[2048,1024]{1,0:T(8,128)(2,1)} %param.2, f32[2048]{0:T(1024)S(1)} %add_rsqrt_fusion, bf16[]{:T(256)} %constant.11.clone.1), kind=kCustom, calls=%fused_computation.10 | custom fusion | flops 6291456 | bytes 12591106 | tf_op jit(solution)/shard_map/scatter | solution.py:37
  67.5 0.0 all-to-all-done
  67.5 10.5 %all-to-all-start.1 = ((bf16[64,64,1024]{2,1,0:T(8,128)(2,1)}), bf16[64,64,1024]{2,1,0:T(8,128)(2,1)}, u32[]{:S(2)}, u32[]{:S(2)}) async-start(bf16[64,64,1024]{2,1,0:T(8,128)(2,1)} %bitcast.24), calls=%async_computation.1 | async-start | bytes 16777216 | tf_op jit(solution)/shard_map/all_to_all | solution.py:41
  78.0 0.1 reduce
  78.1 0.1 reshape.52
  78.2 0.1 dynamic-slice_compare_fusion
  78.2 182.1 %all-to-all-done.1 = bf16[64,64,1024]{2,1,0:T(8,128)(2,1)} async-done(((bf16[64,64,1024]{2,1,0:T(8,128)(2,1)}), bf16[64,64,1024]{2,1,0:T(8,128)(2,1)}, u32[]{:S(2)}, u32[]{:S(2)}) %all-to-all-start.1) | async-done | bytes 8388640 | tf_op jit(solution)/shard_map/all_to_all | solution.py:41
  260.3 8.9 %select_reduce_fusion = f32[4096]{0:T(1024)S(1)} fusion(bf16[4096,1024]{1,0:T(8,128)(2,1)} %bitcast.5, s32[512]{0:T(512)S(1)} %iota_add_fusion, pred[512]{0:T(512)(128)(4,1)S(1)} %dynamic-slice_compare_fusion, s32[]{:T(128)S(6)} %select_n.14), kind=kOutput, calls=%fused_computation.7 | convolution fusion | flops 4303351808 | bytes 9456132 | tf_op jit(solution)/shard_map/dot_general | solution.py:16
  269.2 0.1 all_to_all.18
  269.3 29.0 %pmax.7 = f32[64,1,64]{2,1,0:T(1,128)S(1)} all-reduce(f32[64,1,64]{2,1,0:T(1,128)S(1)} %all_to_all.18), channel_id=1, replica_groups=mesh['corpus'=64,'tile'=8] {'tile'}, use_global_device_ids=true, to_apply=%region_7.8 | all-reduce | flops 4096 | bytes 32768 | tf_op jit(solution)/shard_map/pmax | solution.py:55
  298.3 26.1 %all_to_all.24 = f32[64,1,64]{2,1,0:T(1,128)S(1)} all-to-all(f32[64,1,64]{2,1,0:T(1,128)S(1)} %pmax.7), channel_id=1, replica_groups=mesh['corpus'=64,'tile'=8] {'corpus'}, dimensions={0} | all-to-all | bytes 32768 | tf_op jit(solution)/shard_map/all_to_all | solution.py:56
  324.5 0.5 broadcast.49
  325.0 0.7 reduce.4
  325.7 0.1 reshape.56
  325.8 20.5 %gather_fusion = f32[2048]{0:T(1024)} fusion(f32[4096]{0:T(1024)S(1)} %reshape.56, s32[2048]{0:T(1024)S(1)} %get-tuple-element.5), kind=kCustom, calls=%fused_computation | custom fusion | bytes 24576 | tf_op jit(solution)/shard_map/gather | solution.py:57
  (3 shorter events, 0.0 us)
Async XLA Ops:
  36.9 30.5 %all-to-all-start = ((bf16[64,1,64]{2,1,0:T(2,128)(2,1)}), bf16[64,1,64]{2,1,0:T(2,128)(2,1)S(1)}, u32[]{:S(2)}, u32[]{:S(2)}) async-start(bf16[64,1,64]{2,1,0:T(2,128)(2,1)} %all_to_all.20), calls=%async_computation | async-start | bytes 65536 | tf_op jit(solution)/shard_map/all_to_all | solution.py:42
  67.5 192.9 %all-to-all-start.1 = ((bf16[64,64,1024]{2,1,0:T(8,128)(2,1)}), bf16[64,64,1024]{2,1,0:T(8,128)(2,1)}, u32[]{:S(2)}, u32[]{:S(2)}) async-start(bf16[64,64,1024]{2,1,0:T(8,128)(2,1)} %bitcast.24), calls=%async_computation.1 | async-start | bytes 16777216 | tf_op jit(solution)/shard_map/all_to_all | solution.py:41
where the time goes:
time: 347 us; the launch traced here: 346 us
  waiting for transfers between devices  182 us (52%)
  blocking collectives  55.2 us (16%)
  other arithmetic  40.8 us (12%)
  local copies, waits for them, and re-layouts  37.2 us (11%)
  starting transfers between devices  22.1 us (6%)
  matrix products  8.88 us (3%)
    all_to_all x1, waiting for transfers between devices, local(): lax.all_to_all(outbox, 'corpus', split_axis=0, concat_axis=0, tiled=True)  182 us
    pmax x1, blocking collectives, local(): partial_value = lax.pmax(partial_value, 'tile')  29 us
    all_to_all x1, blocking collectives, local(): lax.all_to_all(partial_value, 'corpus', split_axis=0, concat_axis=0, tile...  26.1 us
    gather x1, local copies, waits for them, and re-layouts, local(): best = returned.reshape(total)[slot]  20.5 us
    another operation x3, other arithmetic  18.5 us
    scatter x1, other arithmetic, local(): jnp.zeros((total, width), jnp.bfloat16).at[slot].set(unit)  15.8 us
    scatter x1, local copies, waits for them, and re-layouts, local(): jnp.zeros((total,), jnp.bfloat16).at[slot].set(1.0)  14.6 us
    all_to_all x1, starting transfers between devices, local(): lax.all_to_all(filled, 'corpus', split_axis=0, concat_axis=0, tiled=True)  11.6 us
  transfers between devices with their start and end apart: 2, of which 1 were waited for; matrix products, arithmetic and copies ran while one was open for 6% of the time, Pallas kernels for 0%

commit v1 on v0

v1 whole, which is shorter than its diff:
```python
import functools

import jax
import jax.numpy as jnp
from jax import lax
from jax.experimental import pallas as pl
from jax.experimental.pallas import tpu as pltpu
from jax.sharding import PartitionSpec as P

EPS = 1e-06
MESH = pl.DeviceIdType.MESH
NY, NX, NZ = 8, 4, 8
SLOTS = 64
PIECES = 4
PIECE_RANKS = SLOTS // PIECES
PIECE = NY * PIECE_RANKS
UNIT = NY * SLOTS
LANES = 128
MARK = 4.0
NEG = -1e6


def corpus_id(y, x, k):
    return (y * NX + x) * 2 + k


def inner(left, right):
    return lax.dot_general(
        left, right, (((1,), (1,)), ((), ())), preferred_element_type=jnp.float32
    )


def row_bias(unit):
    head = unit[:, :LANES].astype(jnp.float32)
    return jnp.where(head > MARK / 2, jnp.float32(NEG), jnp.float32(0.0))


def lane_bias(unit):
    first = (lax.broadcasted_iota(jnp.int32, (16, LANES), 1) == 0).astype(jnp.bfloat16)
    head = inner(first, unit[:, :LANES])[0:1]
    return jnp.where(head > MARK / 2, jnp.float32(NEG), jnp.float32(0.0))


def kernel(
    emb_hbm, ids_ref, out_ref,
    emb, outbox, obuf, lbuf, rbuf, part_out, part_in, ret_y, ret_z,
    emb_sem, own_sem, ysend, yrecv, fsend, frecv, psend, precv, ry_send, ry_recv, rz_send, rz_recv,
):
    corpus = lax.axis_index("corpus")
    z = lax.axis_index("tile")
    y, x, k = corpus // (NX * 2), (corpus // 2) % NX, corpus % 2
    right, left = (x + 1) % NX, (x + NX - 1) % NX
    right_core = (k + x // 2) % 2
    left_core = (k + left // 2) % 2
    sib = corpus_id(y, x, 1 - k)

    load = pltpu.make_async_copy(emb_hbm, emb, emb_sem)
    load.start()

    barrier = pltpu.get_barrier_semaphore()

    def greet(corpus_to, tile_to):
        pl.semaphore_signal(barrier, inc=1, device_id=(corpus_to, tile_to), device_id_type=MESH)

    for d in range(1, NY):
        greet(corpus_id((y + d) % NY, x, k), z)
    for d in range(1, NZ):
        greet(corpus, (z + d) % NZ)
    for core in range(2):
        greet(corpus_id(y, right, core), z)
        greet(corpus_id(y, left, core), z)
    greet(sib, z)

    ids = ids_ref[...]
    rows = ids.shape[1]
    clusters = NY * NZ
    member = lax.broadcasted_iota(jnp.int32, (clusters, rows), 0) == ids
    onehot = jnp.where(member, jnp.float32(1.0), jnp.float32(0.0)).astype(jnp.bfloat16)
    step = 256
    row_i = lax.broadcasted_iota(jnp.int32, (step, step + LANES), 0)
    col_i = lax.broadcasted_iota(jnp.int32, (step, step + LANES), 1)
    earlier = ((row_i < col_i) | (col_i >= step)).astype(jnp.bfloat16)
    carry = jnp.zeros((clusters, LANES), jnp.float32)
    ranks = []
    for b in range(rows // step):
        part = onehot[:, b * step:(b + 1) * step]
        count = jnp.dot(part, earlier, preferred_element_type=jnp.float32)
        before = count[:, :step] + jnp.concatenate([carry] * (step // LANES), axis=1)
        ranks.append(jnp.sum(before * part.astype(jnp.float32), axis=0, keepdims=True))
        carry = carry + count[:, step:]
    rank = jnp.concatenate(ranks, axis=1)
    key = (ids - z * NY) * SLOTS + rank.astype(jnp.int32)

    load.wait()

    def y_copy(d, p):
        to = (y + d) % NY
        return pltpu.make_async_remote_copy(
            src_ref=outbox.at[p, to],
            dst_ref=obuf.at[0, pl.ds(pl.multiple_of(p * PIECE + y * PIECE_RANKS, 16), PIECE_RANKS)],
            send_sem=ysend.at[p, d],
            recv_sem=yrecv.at[p, d],
            device_id=(corpus_id(to, x, k), z),
            device_id_type=MESH,
        )

    def y_arrival(d, p):
        source = (y + NY - d) % NY
        return pltpu.make_async_remote_copy(
            src_ref=outbox.at[p, source],
            dst_ref=obuf.at[0, pl.ds(pl.multiple_of(p * PIECE + source * PIECE_RANKS, 16), PIECE_RANKS)],
            send_sem=ysend.at[p, d],
            recv_sem=yrecv.at[p, d],
            device_id=(corpus_id(source, x, k), z),
            device_id_type=MESH,
        )

    def own_copy(p):
        return pltpu.make_async_copy(
            outbox.at[p, y],
            obuf.at[0, pl.ds(pl.multiple_of(p * PIECE + y * PIECE_RANKS, 16), PIECE_RANKS)],
            own_sem.at[p],
        )

    order = (4, 3, 5, 2, 6, 1, 7)
    slot_i = lax.broadcasted_iota(jnp.int32, (PIECE, 1), 0)
    lane_i = lax.broadcasted_iota(jnp.int32, (PIECE, emb.shape[1]), 1)
    for p in range(PIECES):
        wanted = (slot_i // PIECE_RANKS) * SLOTS + p * PIECE_RANKS + slot_i % PIECE_RANKS
        pick = jnp.where(wanted == key, jnp.float32(1.0), jnp.float32(0.0))
        filled = jnp.sum(pick, axis=1, keepdims=True)
        values = jnp.dot(pick.astype(jnp.bfloat16), emb[...], preferred_element_type=jnp.float32)
        total = jnp.sum(values * values, axis=1, keepdims=True)
        empty = jnp.where(lane_i < LANES, jnp.float32(MARK), jnp.float32(0.0))
        unit = jnp.where(filled > 0.5, values * lax.rsqrt(total + EPS), empty)
        outbox[p] = unit.astype(jnp.bfloat16).reshape(NY, PIECE_RANKS, emb.shape[1])
        if p == 0:
            pl.semaphore_wait(barrier, NY - 1 + NZ - 1 + 5)
        for d in order:
            y_copy(d, p).start()
        own_copy(p).start()

    def forward(p, way):
        there = pl.ds(p * PIECE, PIECE)
        target, to = (
            (lbuf.at[there], corpus_id(y, right, k)),
            (rbuf.at[there], corpus_id(y, left, left_core)),
            (obuf.at[1, there], sib),
        )[way]
        return pltpu.make_async_remote_copy(
            src_ref=obuf.at[0, there],
            dst_ref=target,
            send_sem=fsend.at[p, way],
            recv_sem=frecv.at[p, way],
            device_id=(to, z),
            device_id_type=MESH,
        )

    for p in range(PIECES):
        own_copy(p).wait()
        for d in order:
            y_arrival(d, p).wait_recv()
        for way in range(3):
            forward(p, way).start()

    half = UNIT // 2

    def scores(left_unit, right_ref, n):
        return inner(left_unit, right_ref[n * half:(n + 1) * half])

    def wide(bias):
        return jnp.concatenate([bias] * (half // LANES), axis=1)

    def col_max(s, bias):
        return jnp.max(s + wide(bias), axis=0, keepdims=True)

    def row_max(s, bias_row, n):
        shifted = s + bias_row[:, n * half:(n + 1) * half]
        return jnp.maximum(shifted[:, :LANES], shifted[:, LANES:])

    def to_lanes(m):
        return jnp.max(m.T, axis=0, keepdims=True)

    own = obuf.at[0]
    own_unit = own[...]
    own_rows, own_lanes = row_bias(own_unit), lane_bias(own_unit)
    best = []
    for n in range(2):
        s = scores(own_unit, own, n)
        same = lax.broadcasted_iota(jnp.int32, s.shape, 0) == (
            lax.broadcasted_iota(jnp.int32, s.shape, 1) + n * half
        )
        best.append(col_max(jnp.where(same, jnp.float32(NEG), s), own_rows))
    own_best = jnp.concatenate(best, axis=1)

    for p in range(PIECES):
        forward(p, 2).wait_recv()
    sib_unit = obuf[1]
    sib_rows = row_bias(sib_unit)
    own_best = jnp.maximum(
        own_best,
        jnp.concatenate([col_max(scores(sib_unit, own, n), sib_rows) for n in range(2)], axis=1),
    )

    which = 1 - left // 2
    for p in range(PIECES):
        forward(p, 0).wait_recv()
    left_unit = lbuf[...]
    left_rows, left_lanes = row_bias(left_unit), lane_bias(left_unit)
    beside = obuf.at[which]
    beside_lanes = lane_bias(beside[...])
    best, left_acc = [], None
    for n in range(2):
        s = scores(left_unit, beside, n)
        best.append(col_max(s, left_rows))
        acc = row_max(s, beside_lanes, n)
        left_acc = acc if left_acc is None else jnp.maximum(left_acc, acc)
    beside_best = jnp.concatenate(best, axis=1)
    beside_own = which.astype(jnp.float32)
    own_best = jnp.maximum(own_best, beside_best + beside_own * NEG)
    sib_best = beside_best + (1.0 - beside_own) * NEG

    for p in range(PIECES):
        forward(p, 1).wait_recv()
    right_unit = rbuf[...]
    right_rows, right_lanes = row_bias(right_unit), lane_bias(right_unit)
    best, right_acc = [], None
    for n in range(2):
        s = scores(right_unit, own, n)
        best.append(col_max(s, right_rows))
        acc = row_max(s, own_lanes, n)
        right_acc = acc if right_acc is None else jnp.maximum(right_acc, acc)
    own_best = jnp.maximum(own_best, jnp.concatenate(best, axis=1))

    best = []
    for n in range(2):
        s = scores(left_unit, rbuf, n)
        best.append(col_max(s, left_rows))
        left_acc = jnp.maximum(left_acc, row_max(s, right_lanes, n))
    right_best = jnp.maximum(jnp.concatenate(best, axis=1), to_lanes(right_acc))
    left_best = to_lanes(left_acc)

    def give(way):
        to = (corpus_id(y, left, k), corpus_id(y, right, right_core), sib)[way]
        return pltpu.make_async_remote_copy(
            src_ref=part_out.at[way],
            dst_ref=part_in.at[way],
            send_sem=psend.at[way],
            recv_sem=precv.at[way],
            device_id=(to, z),
            device_id_type=MESH,
        )

    def as_tile(v):
        pieces = [v[:, i * LANES:(i + 1) * LANES] for i in range(UNIT // LANES)]
        return jnp.concatenate(pieces + [jnp.zeros((8 - len(pieces), LANES), jnp.float32)], axis=0)

    for way, v in ((1, right_best), (0, left_best), (2, sib_best)):
        part_out[way] = as_tile(v)
        give(way).start()
    final = jnp.maximum(as_tile(own_best), -1.0)
    for way in range(3):
        give(way).wait_recv()
        final = jnp.maximum(final, part_in[way])

    ret_y[y] = final

    def back_y(d, received):
        at = (y + NY - d) % NY if received else y
        return pltpu.make_async_remote_copy(
            src_ref=ret_y.at[at],
            dst_ref=ret_y.at[at],
            send_sem=ry_send.at[d],
            recv_sem=ry_recv.at[d],
            device_id=(corpus_id((y + d) % NY, x, k), z),
            device_id_type=MESH,
        )

    for d in order:
        back_y(d, False).start()
    for d in order:
        back_y(d, True).wait_recv()
    lane = lax.broadcasted_iota(jnp.int32, (NY, LANES), 1)
    mine = jnp.zeros((NY, LANES), jnp.float32)
    for p in range(PIECES):
        shift = (p * PIECE_RANKS - y * PIECE_RANKS + LANES) % LANES
        turned = pltpu.roll(ret_y[:, p, :], shift, 1)
        mine = jnp.where(lane // PIECE_RANKS == p, turned, mine)

    ret_z[z] = mine

    def back_z(d, received):
        at = (z + NZ - d) % NZ if received else z
        return pltpu.make_async_remote_copy(
            src_ref=ret_z.at[at],
            dst_ref=ret_z.at[at],
            send_sem=rz_send.at[d],
            recv_sem=rz_recv.at[d],
            device_id=(corpus, (z + d) % NZ),
            device_id_type=MESH,
        )

    for d in order:
        back_z(d, False).start()
    for d in order:
        back_z(d, True).wait_recv()

    table = ret_z[...].reshape(clusters, LANES)
    found = jnp.zeros((LANES, rows), jnp.float32)
    for _ in range(3):
        rounded = table.astype(jnp.bfloat16)
        table = table - rounded.astype(jnp.float32)
        found = found + lax.dot_general(
            rounded, onehot, (((0,), (0,)), ((), ())), preferred_element_type=jnp.float32
        )
    rank_i = lax.broadcasted_iota(jnp.int32, (SLOTS, rows), 0)
    hit = rank_i == rank.astype(jnp.int32)
    out_ref[...] = jnp.sum(jnp.where(hit, found[:SLOTS], 0.0), axis=0, keepdims=True)

    for p in range(PIECES):
        for d in order:
            y_copy(d, p).wait_send()
        for way in range(3):
            forward(p, way).wait_send()
    for way in range(3):
        give(way).wait_send()
    for d in order:
        back_y(d, False).wait_send()
        back_z(d, False).wait_send()


def local(embeddings, cluster_ids):
    rows, width = embeddings.shape
    dma = pltpu.SemaphoreType.DMA
    best = pl.pallas_call(
        kernel,
        out_shape=jax.ShapeDtypeStruct((1, rows), jnp.float32),
        in_specs=[pl.BlockSpec(memory_space=pl.ANY), pl.BlockSpec(memory_space=pltpu.VMEM)],
        out_specs=pl.BlockSpec(memory_space=pltpu.VMEM),
        scratch_shapes=[
            pltpu.VMEM((rows, width), jnp.bfloat16),
            pltpu.VMEM((PIECES, NY, PIECE_RANKS, width), jnp.bfloat16),
            pltpu.VMEM((2, UNIT, width), jnp.bfloat16),
            pltpu.VMEM((UNIT, width), jnp.bfloat16),
            pltpu.VMEM((UNIT, width), jnp.bfloat16),
            pltpu.VMEM((3, 8, LANES), jnp.float32),
            pltpu.VMEM((3, 8, LANES), jnp.float32),
            pltpu.VMEM((NY, 8, LANES), jnp.float32),
            pltpu.VMEM((NZ, NY, LANES), jnp.float32),
            dma,
            dma((PIECES,)),
            dma((PIECES, NY)), dma((PIECES, NY)),
            dma((PIECES, 3)), dma((PIECES, 3)),
            dma((3,)), dma((3,)),
            dma((NY,)), dma((NY,)),
            dma((NZ,)), dma((NZ,)),
        ],
        compiler_params=pltpu.CompilerParams(
            collective_id=0, has_side_effects=True, vmem_limit_bytes=48 * 2 ** 20
        ),
        name="cluster_best",
    )(embeddings, cluster_ids.reshape(1, rows))
    return best.reshape(rows)


def solution(mesh):
    in_specs = (P("corpus", None), P("corpus"))
    out_specs = P("corpus")
    return jax.shard_map(local, mesh=mesh, in_specs=in_specs, out_specs=out_specs, check_vma=False)
```

time: 347 us -> 65.9 us (0.19)
  waiting for transfers between devices: 182 us -> 0 us
  Pallas kernels: 0 us -> 61.6 us
  blocking collectives: 55.2 us -> 0 us
  other arithmetic: 40.8 us -> 0 us
  local copies, waits for them, and re-layouts: 37.2 us -> 3.48 us
  starting transfers between devices: 22.1 us -> 0 us
  matrix products: 8.88 us -> 0 us
    all_to_all x2 -> x0, waiting for transfers between devices: 182 us -> none  [the longest x1 182 us: local(): lax.all_to_all(outbox, 'corpus', split_axis=0, concat_axis=0, tiled=True)]
    pallas_call x0 -> x1, Pallas kernels: none -> 61.6 us  [local(): pl.pallas_call(kernel, out_shape=jax.ShapeDtypeStruct((1, rows), jnp.floa...]
    pmax x1 -> x0, blocking collectives: 29 us -> none  [local(): partial_value = lax.pmax(partial_value, 'tile')]
    all_to_all x1 -> x0, blocking collectives: 26.1 us -> none  [local(): lax.all_to_all(partial_value, 'corpus', split_axis=0, concat_axis=0, tile...]
    all_to_all x2 -> x0, starting transfers between devices: 22.1 us -> none  [the longest x1 11.6 us: local(): lax.all_to_all(filled, 'corpus', split_axis=0, concat_axis=0, tiled=True)]
    gather x1 -> x0, local copies, waits for them, and re-layouts: 20.5 us -> none  [local(): best = returned.reshape(total)[slot]]
    another operation x3 -> x0, other arithmetic: 18.5 us -> none
    scatter x1 -> x0, other arithmetic: 15.8 us -> none  [local(): jnp.zeros((total, width), jnp.bfloat16).at[slot].set(unit)]
  transfers between devices with their start and end apart: 2 -> 0, of which waited for: 1 -> 0; matrix products, arithmetic and copies ran while one was open for 6% -> 0% of each run, Pallas kernels for 0% -> 0%
where the time goes in v1:
time: 65.9 us; the launch traced here: 65.1 us
  Pallas kernels  61.6 us (93%)
  local copies, waits for them, and re-layouts  3.48 us (5%)
    pallas_call x1, Pallas kernels, local(): pl.pallas_call(kernel, out_shape=jax.ShapeDtypeStruct((1, rows), jnp.floa...  61.6 us
    unnamed x5, local copies, waits for them, and re-layouts  3.48 us

profile of v1, /device:TPU:1, one launch (start us, length us, event | category | flops | bytes accessed | tf_op | source)
XLA Modules:
  0.0 65.1 jit_solution(5594198233714369090)
XLA Ops:
  0.0 0.0 copy-start
  0.0 2.2 %copy-done = bf16[2048,1024]{1,0:T(8,128)(2,1)S(1)} copy-done((bf16[2048,1024]{1,0:T(8,128)(2,1)S(1)}, bf16[2048,1024]{1,0:T(8,128)(2,1)}, u32[]{:S(2)}) %copy-start) | copy-done | bytes 4194328
  2.2 0.0 copy-start.1
  2.2 0.7 %copy-done.1 = s32[2048]{0:T(1024)S(1)} copy-done((s32[2048]{0:T(1024)S(1)}, s32[2048]{0:T(1024)}, u32[]{:S(2)}) %copy-start.1) | copy-done | bytes 8216
  2.9 61.6 %cluster_best.1 = f32[1,2048]{1,0:T(1,128)S(1)} custom-call(bf16[2048,1024]{1,0:T(8,128)(2,1)S(1)} %copy-done, s32[1,2048]{1,0:T(1,128)S(1)} %bitcast.3), custom_call_target="tpu_custom_call" | custom-call | tf_op jit(solution)/shard_map/cluster_best/pallas_call | solution.py:335
  64.5 0.6 copy.4
Async XLA Ops:
  0.0 2.2 %copy-start = (bf16[2048,1024]{1,0:T(8,128)(2,1)S(1)}, bf16[2048,1024]{1,0:T(8,128)(2,1)}, u32[]{:S(2)}) copy-start(bf16[2048,1024]{1,0:T(8,128)(2,1)} %emb_hbm.1) | copy-start | bytes 12582916
  2.2 0.7 %copy-start.1 = (s32[2048]{0:T(1024)S(1)}, s32[2048]{0:T(1024)}, u32[]{:S(2)}) copy-start(s32[2048]{0:T(1024)} %param.3) | copy-start | bytes 24580

commit v2 on v1

v2 whole, which is shorter than its diff:
```python
import functools

import jax
import jax.numpy as jnp
from jax import lax
from jax.experimental import pallas as pl
from jax.experimental.pallas import tpu as pltpu
from jax.sharding import PartitionSpec as P

EPS = 1e-06
MESH = pl.DeviceIdType.MESH
NY, NX, NZ = 8, 4, 8
SLOTS = 64
PIECES = 4
PIECE_RANKS = SLOTS // PIECES
PIECE = NY * PIECE_RANKS
UNIT = NY * SLOTS
LANES = 128
MARK = 4.0
NEG = -1e6
HALF = UNIT // 2
SEND_ORDER = (4, 3, 5, 2, 6, 1, 7)
ARRIVAL_ORDER = SEND_ORDER


def corpus_id(y, x, k):
    return (y * NX + x) * 2 + k


def inner(left, right):
    return lax.dot_general(
        left, right, (((1,), (1,)), ((), ())), preferred_element_type=jnp.float32
    )


def row_bias(unit):
    head = unit[:, :LANES].astype(jnp.float32)
    return jnp.where(head > MARK / 2, jnp.float32(NEG), jnp.float32(0.0))


def lane_bias(unit):
    first = (lax.broadcasted_iota(jnp.int32, (16, LANES), 1) == 0).astype(jnp.bfloat16)
    head = inner(first, unit[:, :LANES])[0:1]
    return jnp.where(head > MARK / 2, jnp.float32(NEG), jnp.float32(0.0))


def kernel(
    emb_hbm, ids_hbm, out_ref,
    emb, ids_ref, counts, outbox, obuf, lbuf, rbuf, part_out, part_in, ret_y, ret_z,
    emb_sem, ids_sem, own_sem, ysend, yrecv, fsend, frecv, psend, precv,
    ry_send, ry_recv, rz_send, rz_recv,
):
    corpus = lax.axis_index("corpus")
    z = lax.axis_index("tile")
    y, x, k = corpus // (NX * 2), (corpus // 2) % NX, corpus % 2
    right, left = (x + 1) % NX, (x + NX - 1) % NX
    right_core = (k + x // 2) % 2
    left_core = (k + left // 2) % 2
    sib = corpus_id(y, x, 1 - k)
    rows, width = emb.shape

    ids_load = pltpu.make_async_copy(ids_hbm, ids_ref, ids_sem)
    ids_load.start()
    load = pltpu.make_async_copy(emb_hbm, emb, emb_sem)
    load.start()

    barrier = pltpu.get_barrier_semaphore()

    def greet(corpus_to, tile_to):
        pl.semaphore_signal(barrier, inc=1, device_id=(corpus_to, tile_to), device_id_type=MESH)

    for d in range(1, NY):
        greet(corpus_id((y + d) % NY, x, k), z)
    for core in range(2):
        greet(corpus_id(y, right, core), z)
        greet(corpus_id(y, left, core), z)
    greet(sib, z)
    for d in range(1, NZ):
        greet(corpus, (z + d) % NZ)

    ids_load.wait()
    ids = ids_ref[...]
    clusters = NY * NZ
    member = lax.broadcasted_iota(jnp.int32, (clusters, rows), 0) == ids
    onehot = jnp.where(member, jnp.float32(1.0), jnp.float32(0.0)).astype(jnp.bfloat16)
    step = 256
    row_i = lax.broadcasted_iota(jnp.int32, (step, step + LANES), 0)
    col_i = lax.broadcasted_iota(jnp.int32, (step, step + LANES), 1)
    earlier = ((row_i < col_i) | (col_i >= step)).astype(jnp.bfloat16)
    carry = jnp.zeros((clusters, LANES), jnp.float32)
    ranks = []
    for b in range(rows // step):
        part = onehot[:, b * step:(b + 1) * step]
        count = jnp.dot(part, earlier, preferred_element_type=jnp.float32)
        before = count[:, :step] + jnp.concatenate([carry] * (step // LANES), axis=1)
        ranks.append(jnp.sum(before * part.astype(jnp.float32), axis=0, keepdims=True))
        carry = carry + count[:, step:]
    rank = jnp.concatenate(ranks, axis=1)
    counts[...] = carry
    key = (ids - z * NY) * SLOTS + rank.astype(jnp.int32)

    def block_rows(p, source):
        return pl.ds(pl.multiple_of(p * PIECE + source * PIECE_RANKS, 16), PIECE_RANKS)

    def y_copy(d, p):
        to = (y + d) % NY
        return pltpu.make_async_remote_copy(
            src_ref=outbox.at[p, to],
            dst_ref=obuf.at[0, block_rows(p, y)],
            send_sem=ysend.at[p, d],
            recv_sem=yrecv.at[p, d],
            device_id=(corpus_id(to, x, k), z),
            device_id_type=MESH,
        )

    def y_arrival(d, p):
        source = (y + NY - d) % NY
        return pltpu.make_async_remote_copy(
            src_ref=outbox.at[p, source],
            dst_ref=obuf.at[0, block_rows(p, source)],
            send_sem=ysend.at[p, d],
            recv_sem=yrecv.at[p, d],
            device_id=(corpus_id(source, x, k), z),
            device_id_type=MESH,
        )

    def own_copy(p):
        return pltpu.make_async_copy(outbox.at[p, y], obuf.at[0, block_rows(p, y)], own_sem.at[p])

    def forward(p, way, source=None):
        there = pl.ds(p * PIECE, PIECE) if source is None else block_rows(p, source)
        target, to = (
            (lbuf.at[there], corpus_id(y, right, k)),
            (rbuf.at[there], corpus_id(y, left, left_core)),
            (obuf.at[1, there], sib),
        )[way]
        return pltpu.make_async_remote_copy(
            src_ref=obuf.at[0, there],
            dst_ref=target,
            send_sem=fsend.at[p, way],
            recv_sem=frecv.at[p, way],
            device_id=(to, z),
            device_id_type=MESH,
        )

    live = counts[pl.ds(pl.multiple_of(z * NY, 8), NY), :]
    live = jnp.broadcast_to(live[:, None, :], (NY, PIECE_RANKS, LANES)).reshape(PIECE, LANES)
    rank_i = (lax.broadcasted_iota(jnp.int32, (PIECE, LANES), 0) % PIECE_RANKS).astype(jnp.float32)
    slot_i = lax.broadcasted_iota(jnp.int32, (PIECE, 1), 0)
    load.wait()
    for p in range(PIECES):
        wanted = (slot_i // PIECE_RANKS) * SLOTS + p * PIECE_RANKS + slot_i % PIECE_RANKS
        pick = jnp.where(wanted == key, jnp.float32(1.0), jnp.float32(0.0)).astype(jnp.bfloat16)
        values = jnp.dot(pick, emb[...], preferred_element_type=jnp.float32)
        scale = lax.rsqrt(jnp.sum(values * values, axis=1, keepdims=True) + EPS)
        filled = rank_i + p * PIECE_RANKS < live
        head = jnp.where(filled, values[:, :LANES] * scale, jnp.float32(MARK))
        unit = jnp.concatenate([head, values[:, LANES:] * scale], axis=1)
        outbox[p] = unit.astype(jnp.bfloat16).reshape(NY, PIECE_RANKS, width)
        if p == 0:
            pl.semaphore_wait(barrier, NY - 1 + NZ - 1 + 5)
        for d in SEND_ORDER:
            y_copy(d, p).start()
        own_copy(p).start()

    for p in range(PIECES):
        own_copy(p).wait()
        for way in range(3):
            forward(p, way, y).start()
    for p in range(PIECES):
        for d in ARRIVAL_ORDER:
            y_arrival(d, p).wait_recv()
            for way in range(3):
                forward(p, way, (y + NY - d) % NY).start()

    def col_max(s, bias):
        bias = jnp.concatenate([bias] * (s.shape[1] // LANES), axis=1)
        return jnp.max(s + bias, axis=0, keepdims=True)

    def row_max(s, bias):
        s = s + bias
        best = s[:, :LANES]
        for i in range(1, s.shape[1] // LANES):
            best = jnp.maximum(best, s[:, i * LANES:(i + 1) * LANES])
        return best

    def to_lanes(m):
        return jnp.max(m.T, axis=0, keepdims=True)

    def half(ref, h):
        return ref[h * HALF:(h + 1) * HALF]

    def await_half(h, way):
        for p in range(h * PIECES // 2, (h + 1) * PIECES // 2):
            forward(p, way).wait_recv()

    own_unit = obuf[0]
    own_rows, own_lanes = row_bias(own_unit), lane_bias(own_unit)
    own_best = jnp.full((1, UNIT), NEG, jnp.float32)
    for h in range(2):
        s = inner(half(own_unit, h), own_unit)
        same = lax.broadcasted_iota(jnp.int32, s.shape, 0) + h * HALF == (
            lax.broadcasted_iota(jnp.int32, s.shape, 1)
        )
        best = col_max(jnp.where(same, jnp.float32(NEG), s), half(own_rows, h))
        own_best = jnp.maximum(own_best, best)

    for h in range(2):
        await_half(h, 2)
        sib_half = obuf[1, h * HALF:(h + 1) * HALF]
        best = col_max(inner(sib_half, own_unit), row_bias(sib_half))
        own_best = jnp.maximum(own_best, best)

    which = 1 - left // 2
    beside = obuf[which]
    beside_lanes = lane_bias(beside)
    beside_best = jnp.full((1, UNIT), NEG, jnp.float32)
    left_best, right_best, left_lanes, right_lanes = [], [], [], []
    for h in range(2):
        await_half(h, 0)
        left_half = half(lbuf, h)
        left_rows = row_bias(left_half)
        left_lanes.append(lane_bias(left_half))
        s = inner(left_half, beside)
        beside_best = jnp.maximum(beside_best, col_max(s, left_rows))
        left_acc = row_max(s, beside_lanes)

        await_half(h, 1)
        right_half = half(rbuf, h)
        right_rows = row_bias(right_half)
        right_lanes.append(lane_bias(right_half))
        s = inner(right_half, own_unit)
        own_best = jnp.maximum(own_best, col_max(s, right_rows))
        right_acc = row_max(s, own_lanes)

        s = inner(left_half, rbuf[:(h + 1) * HALF])
        left_acc = jnp.maximum(left_acc, row_max(s, jnp.concatenate(right_lanes, axis=1)))
        best = col_max(s, left_rows)
        for g in range(h):
            right_best[g] = jnp.maximum(right_best[g], best[:, g * HALF:(g + 1) * HALF])
        right_best.append(best[:, h * HALF:])
        if h > 0:
            s = inner(right_half, lbuf[:h * HALF])
            right_acc = jnp.maximum(right_acc, row_max(s, jnp.concatenate(left_lanes[:h], axis=1)))
            best = col_max(s, right_rows)
            for g in range(h):
                left_best[g] = jnp.maximum(left_best[g], best[:, g * HALF:(g + 1) * HALF])
        left_best.append(to_lanes(left_acc))
        right_best[h] = jnp.maximum(right_best[h], to_lanes(right_acc))
    left_best = jnp.concatenate(left_best, axis=1)
    right_best = jnp.concatenate(right_best, axis=1)
    beside_own = which.astype(jnp.float32)
    own_best = jnp.maximum(own_best, beside_best + beside_own * NEG)
    sib_best = beside_best + (1.0 - beside_own) * NEG

    def give(way):
        to = (corpus_id(y, left, k), corpus_id(y, right, right_core), sib)[way]
        return pltpu.make_async_remote_copy(
            src_ref=part_out.at[way],
            dst_ref=part_in.at[way],
            send_sem=psend.at[way],
            recv_sem=precv.at[way],
            device_id=(to, z),
            device_id_type=MESH,
        )

    def as_tile(v):
        pieces = [v[:, i * LANES:(i + 1) * LANES] for i in range(UNIT // LANES)]
        return jnp.concatenate(pieces + [jnp.zeros((8 - len(pieces), LANES), jnp.float32)], axis=0)

    for way, v in ((1, right_best), (0, left_best), (2, sib_best)):
        part_out[way] = as_tile(v)
        give(way).start()
    final = jnp.maximum(as_tile(own_best), -1.0)
    for way in range(3):
        give(way).wait_recv()
        final = jnp.maximum(final, part_in[way])

    ret_y[y] = final

    def back_y(d, received):
        at = (y + NY - d) % NY if received else y
        return pltpu.make_async_remote_copy(
            src_ref=ret_y.at[at],
            dst_ref=ret_y.at[at],
            send_sem=ry_send.at[d],
            recv_sem=ry_recv.at[d],
            device_id=(corpus_id((y + d) % NY, x, k), z),
            device_id_type=MESH,
        )

    for d in SEND_ORDER:
        back_y(d, False).start()
    for d in SEND_ORDER:
        back_y(d, True).wait_recv()
    lane = lax.broadcasted_iota(jnp.int32, (NY, LANES), 1)
    mine = jnp.zeros((NY, LANES), jnp.float32)
    for p in range(PIECES):
        shift = (p * PIECE_RANKS - y * PIECE_RANKS + LANES) % LANES
        turned = pltpu.roll(ret_y[:, p, :], shift, 1)
        mine = jnp.where(lane // PIECE_RANKS == p, turned, mine)

    ret_z[z] = mine

    def back_z(d, received):
        at = (z + NZ - d) % NZ if received else z
        return pltpu.make_async_remote_copy(
            src_ref=ret_z.at[at],
            dst_ref=ret_z.at[at],
            send_sem=rz_send.at[d],
            recv_sem=rz_recv.at[d],
            device_id=(corpus, (z + d) % NZ),
            device_id_type=MESH,
        )

    for d in SEND_ORDER:
        back_z(d, False).start()
    for d in SEND_ORDER:
        back_z(d, True).wait_recv()

    table = ret_z[...].reshape(clusters, LANES)
    found = jnp.zeros((LANES, rows), jnp.float32)
    for _ in range(3):
        rounded = table.astype(jnp.bfloat16)
        table = table - rounded.astype(jnp.float32)
        found = found + lax.dot_general(
            rounded, onehot, (((0,), (0,)), ((), ())), preferred_element_type=jnp.float32
        )
    rank_i = lax.broadcasted_iota(jnp.int32, (SLOTS, rows), 0)
    hit = rank_i == rank.astype(jnp.int32)
    out_ref[...] = jnp.sum(jnp.where(hit, found[:SLOTS], 0.0), axis=0, keepdims=True)

    for p in range(PIECES):
        for d in SEND_ORDER:
            y_copy(d, p).wait_send()
        for way in range(3):
            forward(p, way).wait_send()
    for way in range(3):
        give(way).wait_send()
    for d in SEND_ORDER:
        back_y(d, False).wait_send()
        back_z(d, False).wait_send()


def local(embeddings, cluster_ids):
    rows, width = embeddings.shape
    dma = pltpu.SemaphoreType.DMA
    best = pl.pallas_call(
        kernel,
        out_shape=jax.ShapeDtypeStruct((1, rows), jnp.float32),
        in_specs=[pl.BlockSpec(memory_space=pltpu.HBM)] * 2,
        out_specs=pl.BlockSpec(memory_space=pltpu.VMEM),
        scratch_shapes=[
            pltpu.VMEM((rows, width), jnp.bfloat16),
            pltpu.VMEM((1, rows), jnp.int32),
            pltpu.VMEM((NY * NZ, LANES), jnp.float32),
            pltpu.VMEM((PIECES, NY, PIECE_RANKS, width), jnp.bfloat16),
            pltpu.VMEM((2, UNIT, width), jnp.bfloat16),
            pltpu.VMEM((UNIT, width), jnp.bfloat16),
            pltpu.VMEM((UNIT, width), jnp.bfloat16),
            pltpu.VMEM((3, 8, LANES), jnp.float32),
            pltpu.VMEM((3, 8, LANES), jnp.float32),
            pltpu.VMEM((NY, 8, LANES), jnp.float32),
            pltpu.VMEM((NZ, NY, LANES), jnp.float32),
            dma, dma, dma((PIECES,)),
            dma((PIECES, NY)), dma((PIECES, NY)),
            dma((PIECES, 3)), dma((PIECES, 3)),
            dma((3,)), dma((3,)),
            dma((NY,)), dma((NY,)),
            dma((NZ,)), dma((NZ,)),
        ],
        compiler_params=pltpu.CompilerParams(
            collective_id=0, has_side_effects=True, vmem_limit_bytes=52 * 2 ** 20
        ),
        name="cluster_best",
    )(embeddings, cluster_ids.reshape(1, rows))
    return best.reshape(rows)


def solution(mesh):
    in_specs = (P("corpus", None), P("corpus"))
    out_specs = P("corpus")
    return jax.shard_map(local, mesh=mesh, in_specs=in_specs, out_specs=out_specs, check_vma=False)
```

time: 65.9 us -> 59.6 us (0.904)
  Pallas kernels: 61.6 us -> 57.9 us
  local copies, waits for them, and re-layouts: 3.48 us -> 1.3 us
    pallas_call x1, Pallas kernels: 61.6 us -> 57.9 us  [local(): pl.pallas_call(kernel, out_shape=jax.ShapeDtypeStruct((1, rows), jnp.floa...]
    unnamed x5 -> x3, local copies, waits for them, and re-layouts: 3.48 us -> 1.3 us
where the time goes in v2:
time: 59.6 us; the launch traced here: 59.2 us
  Pallas kernels  57.9 us (97%)
  local copies, waits for them, and re-layouts  1.3 us (2%)
    pallas_call x1, Pallas kernels, local(): pl.pallas_call(kernel, out_shape=jax.ShapeDtypeStruct((1, rows), jnp.floa...  57.9 us
    unnamed x3, local copies, waits for them, and re-layouts  1.3 us

profile of v2, /device:TPU:1, one launch (start us, length us, event | category | flops | bytes accessed | tf_op | source)
XLA Modules:
  0.0 59.2 jit_solution(15136094310961621153)
XLA Ops:
  0.0 0.0 copy-start
  0.0 0.7 %copy-done = s32[2048]{0:T(1024)S(1)} copy-done((s32[2048]{0:T(1024)S(1)}, s32[2048]{0:T(1024)}, u32[]{:S(2)}) %copy-start) | copy-done | bytes 8216
  0.7 57.9 %cluster_best.1 = f32[1,2048]{1,0:T(1,128)S(1)} custom-call(bf16[2048,1024]{1,0:T(8,128)(2,1)} %emb_hbm.1, s32[1,2048]{1,0:T(1,128)S(1)} %bitcast.3), custom_call_target="tpu_custom_call" | custom-call | tf_op jit(solution)/shard_map/cluster_best/pallas_call | solution.py:348
  58.6 0.6 %copy.4 = f32[2048]{0:T(1024)} copy(f32[2048]{0:T(1024)S(1)} %bitcast.2) | data formatting | bytes 16384
Async XLA Ops:
  0.0 0.7 %copy-start = (s32[2048]{0:T(1024)S(1)}, s32[2048]{0:T(1024)}, u32[]{:S(2)}) copy-start(s32[2048]{0:T(1024)} %param.3) | copy-start | bytes 24580

commit v3 on v2

v3 whole, which is shorter than its diff:
```python
import functools

import jax
import jax.numpy as jnp
from jax import lax
from jax.experimental import pallas as pl
from jax.experimental.pallas import tpu as pltpu
from jax.sharding import PartitionSpec as P

EPS = 1e-06
MESH = pl.DeviceIdType.MESH
NY, NX, NZ = 8, 4, 8
SLOTS = 64
UNIT = NY * SLOTS
PIECE = 128
PIECES = UNIT // PIECE
FIRST = 3 * PIECE
LANES = 128
MARK = 4.0
NEG = -1e6
ORDER = (0, 1, 7, 2, 6, 3, 5, 4)
PLACE = {d: ORDER.index(d) for d in ORDER}
MESSAGES = (
    [(d, 0, 64) for d in (1, 7, 2, 6)]
    + [(d, at, 32) for at in (0, 32) for d in (3, 5)]
    + [(4, at, 16) for at in (0, 16, 32, 48)]
)


def corpus_id(y, x, k):
    return (y * NX + x) * 2 + k


def inner(left, right):
    return lax.dot_general(
        left, right, (((1,), (1,)), ((), ())), preferred_element_type=jnp.float32
    )


def row_bias(unit):
    head = unit[:, :LANES].astype(jnp.float32)
    return jnp.where(head > MARK / 2, jnp.float32(NEG), jnp.float32(0.0))


def lane_bias(unit):
    first = (lax.broadcasted_iota(jnp.int32, (16, LANES), 1) == 0).astype(jnp.bfloat16)
    head = inner(first, unit[:, :LANES])[0:1]
    return jnp.where(head > MARK / 2, jnp.float32(NEG), jnp.float32(0.0))


def kernel(
    emb_hbm, ids_hbm, out_ref,
    emb, ids_ref, counts, outbox, obuf, lbuf, rbuf, own_t, beside_t, left_t, right_t, part_out, part_in, ret_out, ret_in,
    emb_sem, ids_sem, ysend, yrecv, fsend, frecv, psend, precv,
    ret_send, ret_recv,
):
    corpus = lax.axis_index("corpus")
    z = lax.axis_index("tile")
    y, x, k = corpus // (NX * 2), (corpus // 2) % NX, corpus % 2
    right, left = (x + 1) % NX, (x + NX - 1) % NX
    right_core = (k + x // 2) % 2
    left_core = (k + left // 2) % 2
    sib = corpus_id(y, x, 1 - k)
    rows, width = emb.shape

    ids_load = pltpu.make_async_copy(ids_hbm, ids_ref, ids_sem)
    ids_load.start()
    load = pltpu.make_async_copy(emb_hbm, emb, emb_sem)
    load.start()

    barrier = pltpu.get_barrier_semaphore()

    def greet(corpus_to, tile_to):
        pl.semaphore_signal(barrier, inc=1, device_id=(corpus_to, tile_to), device_id_type=MESH)

    for d in range(1, NY):
        greet(corpus_id((y + d) % NY, x, k), z)
    for core in range(2):
        greet(corpus_id(y, right, core), z)
        greet(corpus_id(y, left, core), z)
    greet(sib, z)
    for d in range(1, NZ):
        greet(corpus, (z + d) % NZ)

    ids_load.wait()
    ids = ids_ref[...]
    clusters = NY * NZ
    member = lax.broadcasted_iota(jnp.int32, (clusters, rows), 0) == ids
    onehot = jnp.where(member, jnp.float32(1.0), jnp.float32(0.0)).astype(jnp.bfloat16)
    step = 256
    row_i = lax.broadcasted_iota(jnp.int32, (step, step + LANES), 0)
    col_i = lax.broadcasted_iota(jnp.int32, (step, step + LANES), 1)
    earlier = ((row_i < col_i) | (col_i >= step)).astype(jnp.bfloat16)
    carry = jnp.zeros((clusters, LANES), jnp.float32)
    ranks = []
    for b in range(rows // step):
        part = onehot[:, b * step:(b + 1) * step]
        count = jnp.dot(part, earlier, preferred_element_type=jnp.float32)
        before = count[:, :step] + jnp.concatenate([carry] * (step // LANES), axis=1)
        ranks.append(jnp.sum(before * part.astype(jnp.float32), axis=0, keepdims=True))
        carry = carry + count[:, step:]
    rank = jnp.concatenate(ranks, axis=1)
    counts[...] = carry
    key = (ids - z * NY) * SLOTS + rank.astype(jnp.int32)

    def y_copy(i):
        d, first, count = MESSAGES[i]
        return pltpu.make_async_remote_copy(
            src_ref=outbox.at[d, pl.ds(first, count)],
            dst_ref=obuf.at[0, pl.ds(PLACE[d] * SLOTS + first, count)],
            send_sem=ysend,
            recv_sem=yrecv.at[i],
            device_id=(corpus_id((y + d) % NY, x, k), z),
            device_id_type=MESH,
        )

    def forward(way, first, count):
        there = pl.ds(first, count)
        target, to = (
            (lbuf.at[there], corpus_id(y, right, k)),
            (rbuf.at[there], corpus_id(y, left, left_core)),
            (obuf.at[1, there], sib),
        )[way]
        return pltpu.make_async_remote_copy(
            src_ref=obuf.at[0, there],
            dst_ref=target,
            send_sem=fsend.at[way],
            recv_sem=frecv.at[first // FIRST, way],
            device_id=(to, z),
            device_id_type=MESH,
        )

    slot_i = lax.broadcasted_iota(jnp.int32, (2 * SLOTS, 1), 0)
    rank_i = lax.broadcasted_iota(jnp.int32, (SLOTS, LANES), 0).astype(jnp.float32)
    load.wait()
    for pair in range(NY // 2):
        dists = ORDER[2 * pair:2 * pair + 2]
        tos = [(y + d) % NY for d in dists]
        wanted = slot_i % SLOTS + SLOTS * jnp.where(slot_i < SLOTS, tos[0], tos[1])
        pick = jnp.where(wanted == key, jnp.float32(1.0), jnp.float32(0.0)).astype(jnp.bfloat16)
        values = jnp.dot(pick, emb[...], preferred_element_type=jnp.float32)
        scale = lax.rsqrt(jnp.sum(values * values, axis=1, keepdims=True) + EPS)
        filled = jnp.concatenate([rank_i < counts[pl.ds(z * NY + to, 1), :] for to in tos], axis=0)
        head = jnp.where(filled, values[:, :LANES] * scale, jnp.float32(MARK))
        unit = jnp.concatenate([head, values[:, LANES:] * scale], axis=1).astype(jnp.bfloat16)
        for i, d in enumerate(dists):
            if d == 0:
                obuf[0, :SLOTS] = unit[i * SLOTS:(i + 1) * SLOTS]
            else:
                outbox[d] = unit[i * SLOTS:(i + 1) * SLOTS]
        if pair == 0:
            pl.semaphore_wait(barrier, NY - 1 + NZ - 1 + 5)
        for i, message in enumerate(MESSAGES):
            if message[0] in dists:
                y_copy(i).start()
        if pair == 0:
            for way in range(3):
                forward(way, 0, SLOTS).start()

    for i, (d, first, count) in enumerate(MESSAGES):
        y_copy(i).wait_recv()
        for way in range(3):
            forward(way, PLACE[d] * SLOTS + first, count).start()

    def col_max(s, bias):
        bias = jnp.concatenate([bias] * (s.shape[1] // LANES), axis=1)
        return jnp.max(s + bias, axis=0, keepdims=True)

    def row_max(s, bias):
        s = s + bias
        best = s[:, :LANES]
        for i in range(1, s.shape[1] // LANES):
            best = jnp.maximum(best, s[:, i * LANES:(i + 1) * LANES])
        return best

    def to_lanes(m):
        return jnp.max(m.T, axis=0, keepdims=True)

    def piece(ref, p):
        return ref[p * PIECE:(p + 1) * PIECE]

    def dot(left, right):
        return jnp.dot(left, right, preferred_element_type=jnp.float32)

    def await_part(part, way):
        forward(way, part * FIRST, UNIT - FIRST if part else FIRST).wait_recv()

    own_unit = obuf[0]
    own_rows, own_lanes = row_bias(own_unit), lane_bias(own_unit)
    for p in range(PIECES):
        own_t[:, p * PIECE:(p + 1) * PIECE] = piece(own_unit, p).T
    own_best = jnp.full((1, UNIT), NEG, jnp.float32)
    for p in range(PIECES):
        s = dot(piece(own_unit, p), own_t[...])
        same = lax.broadcasted_iota(jnp.int32, s.shape, 0) + p * PIECE == (
            lax.broadcasted_iota(jnp.int32, s.shape, 1)
        )
        best = col_max(jnp.where(same, jnp.float32(NEG), s), piece(own_rows, p))
        own_best = jnp.maximum(own_best, best)

    await_part(0, 2)
    await_part(1, 2)
    which = 1 - left // 2
    beside = obuf[which]
    beside_lanes = lane_bias(beside)
    for p in range(PIECES):
        beside_t[:, p * PIECE:(p + 1) * PIECE] = piece(beside, p).T
        sib_piece = obuf[1, p * PIECE:(p + 1) * PIECE]
        best = col_max(dot(sib_piece, own_t[...]), row_bias(sib_piece))
        own_best = jnp.maximum(own_best, best)

    beside_best = jnp.full((1, UNIT), NEG, jnp.float32)
    left_best, right_best, left_lanes, right_lanes = [], [], [], []
    for p in range(PIECES):
        there = slice(p * PIECE, (p + 1) * PIECE)
        if p * PIECE in (0, FIRST):
            await_part(p * PIECE // FIRST, 0)
            await_part(p * PIECE // FIRST, 1)
        left_piece, right_piece = lbuf[there], rbuf[there]
        left_rows, right_rows = row_bias(left_piece), row_bias(right_piece)
        left_lanes.append(lane_bias(left_piece))
        right_lanes.append(lane_bias(right_piece))
        right_t[:, there] = right_piece.T
        if p < PIECES - 1:
            left_t[:, there] = left_piece.T
        s = dot(left_piece, beside_t[...])
        beside_best = jnp.maximum(beside_best, col_max(s, left_rows))
        left_acc = row_max(s, beside_lanes)

        s = dot(right_piece, own_t[...])
        own_best = jnp.maximum(own_best, col_max(s, right_rows))
        right_acc = row_max(s, own_lanes)

        s = dot(left_piece, right_t[:, :(p + 1) * PIECE])
        left_acc = jnp.maximum(left_acc, row_max(s, jnp.concatenate(right_lanes, axis=1)))
        best = col_max(s, left_rows)
        for q in range(p):
            right_best[q] = jnp.maximum(right_best[q], best[:, q * PIECE:(q + 1) * PIECE])
        right_best.append(best[:, p * PIECE:])
        if p > 0:
            s = dot(right_piece, left_t[:, :p * PIECE])
            right_acc = jnp.maximum(right_acc, row_max(s, jnp.concatenate(left_lanes[:p], axis=1)))
            best = col_max(s, right_rows)
            for q in range(p):
                left_best[q] = jnp.maximum(left_best[q], best[:, q * PIECE:(q + 1) * PIECE])
        left_best.append(to_lanes(left_acc))
        right_best[p] = jnp.maximum(right_best[p], to_lanes(right_acc))
    left_best = jnp.concatenate(left_best, axis=1)
    right_best = jnp.concatenate(right_best, axis=1)
    beside_own = which.astype(jnp.float32)
    own_best = jnp.maximum(own_best, beside_best + beside_own * NEG)
    sib_best = beside_best + (1.0 - beside_own) * NEG

    def give(way):
        to = (corpus_id(y, left, k), corpus_id(y, right, right_core), sib)[way]
        return pltpu.make_async_remote_copy(
            src_ref=part_out.at[way],
            dst_ref=part_in.at[way],
            send_sem=psend,
            recv_sem=precv,
            device_id=(to, z),
            device_id_type=MESH,
        )

    def as_tile(v):
        pieces = [v[:, i * LANES:(i + 1) * LANES] for i in range(UNIT // LANES)]
        return jnp.concatenate(pieces + [jnp.zeros((8 - len(pieces), LANES), jnp.float32)], axis=0)

    for way, v in ((1, right_best), (0, left_best), (2, sib_best)):
        part_out[way] = as_tile(v)
        give(way).start()
    final = jnp.maximum(as_tile(own_best), -1.0)

    def whole(ref, send_sem, recv_sem):
        return pltpu.make_async_remote_copy(
            src_ref=ref, dst_ref=ref, send_sem=send_sem, recv_sem=recv_sem,
            device_id=(sib, z), device_id_type=MESH,
        )

    whole(part_in, psend, precv).wait_recv()
    for way in range(3):
        final = jnp.maximum(final, part_in[way])

    home = z * NY + y
    for d in range(NY):
        row = final[PLACE[d] // 2:PLACE[d] // 2 + 1]
        if PLACE[d] % 2:
            row = jnp.concatenate([row[:, SLOTS:], row[:, :SLOTS]], axis=1)
        ret_out[d] = row
        if d == 0:
            ret_in[home] = row
    hops = [(d, e) for d in range(NY) for e in range(NZ) if d or e]
    hops.sort(key=lambda de: -min(de[0], NY - de[0]) - min(de[1], NZ - de[1]))
    for d, e in hops:
        pltpu.make_async_remote_copy(
            src_ref=ret_out.at[d],
            dst_ref=ret_in.at[home],
            send_sem=ret_send,
            recv_sem=ret_recv,
            device_id=(corpus_id((y + NY - d) % NY, x, k), (z + e) % NZ),
            device_id_type=MESH,
        ).start()
    returned = whole(ret_in.at[pl.ds(0, NY * NZ - 1)], ret_send, ret_recv)
    returned.wait_recv()

    table = ret_in[...].reshape(clusters, LANES)[:, :SLOTS]
    found = jnp.zeros((SLOTS, rows), jnp.float32)
    for _ in range(3):
        rounded = table.astype(jnp.bfloat16)
        table = table - rounded.astype(jnp.float32)
        found = found + lax.dot_general(
            rounded, onehot, (((0,), (0,)), ((), ())), preferred_element_type=jnp.float32
        )
    rank_i = lax.broadcasted_iota(jnp.int32, (SLOTS, rows), 0)
    hit = rank_i == rank.astype(jnp.int32)
    out_ref[...] = jnp.sum(jnp.where(hit, found, 0.0), axis=0, keepdims=True)

    whole(outbox.at[pl.ds(1, NY - 1)], ysend, ysend).wait_send()
    for way in range(3):
        whole(obuf.at[0], fsend.at[way], fsend.at[way]).wait_send()
    whole(part_out, psend, precv).wait_send()
    returned.wait_send()


def local(embeddings, cluster_ids):
    rows, width = embeddings.shape
    dma = pltpu.SemaphoreType.DMA
    best = pl.pallas_call(
        kernel,
        out_shape=jax.ShapeDtypeStruct((1, rows), jnp.float32),
        in_specs=[pl.BlockSpec(memory_space=pltpu.HBM)] * 2,
        out_specs=pl.BlockSpec(memory_space=pltpu.VMEM),
        scratch_shapes=[
            pltpu.VMEM((rows, width), jnp.bfloat16),
            pltpu.VMEM((1, rows), jnp.int32),
            pltpu.VMEM((NY * NZ, LANES), jnp.float32),
            pltpu.VMEM((NY, SLOTS, width), jnp.bfloat16),
            pltpu.VMEM((2, UNIT, width), jnp.bfloat16),
            pltpu.VMEM((UNIT, width), jnp.bfloat16),
            pltpu.VMEM((UNIT, width), jnp.bfloat16),
            *[pltpu.VMEM((width, UNIT), jnp.bfloat16)] * 4,
            pltpu.VMEM((3, 8, LANES), jnp.float32),
            pltpu.VMEM((3, 8, LANES), jnp.float32),
            pltpu.VMEM((NY, 1, LANES), jnp.float32),
            pltpu.VMEM((NY * NZ, 1, LANES), jnp.float32),
            dma, dma,
            dma, dma((len(MESSAGES),)),
            dma((3,)), dma((2, 3)),
            dma, dma, dma, dma,
        ],
        compiler_params=pltpu.CompilerParams(
            collective_id=0, has_side_effects=True, vmem_limit_bytes=52 * 2 ** 20
        ),
        name="cluster_best",
    )(embeddings, cluster_ids.reshape(1, rows))
    return best.reshape(rows)


def solution(mesh):
    in_specs = (P("corpus", None), P("corpus"))
    out_specs = P("corpus")
    return jax.shard_map(local, mesh=mesh, in_specs=in_specs, out_specs=out_specs, check_vma=False)
```

time: 59.6 us -> 57.2 us (0.960)
  Pallas kernels: 57.9 us -> 55.7 us
    pallas_call x1, Pallas kernels: 57.9 us -> 55.7 us  [local(): pl.pallas_call(kernel, out_shape=jax.ShapeDtypeStruct((1, rows), jnp.floa...]
where the time goes in v3:
time: 57.2 us; the launch traced here: 57 us
  Pallas kernels  55.7 us (97%)
  local copies, waits for them, and re-layouts  1.3 us (2%)
    pallas_call x1, Pallas kernels, local(): pl.pallas_call(kernel, out_shape=jax.ShapeDtypeStruct((1, rows), jnp.floa...  55.7 us
    unnamed x3, local copies, waits for them, and re-layouts  1.3 us

profile of v3, /device:TPU:1, one launch (start us, length us, event | category | flops | bytes accessed | tf_op | source)
XLA Modules:
  0.0 57.0 jit_solution(11589586629496881838)
XLA Ops:
  0.0 0.0 copy-start
  0.0 0.7 %copy-done = s32[2048]{0:T(1024)S(1)} copy-done((s32[2048]{0:T(1024)S(1)}, s32[2048]{0:T(1024)}, u32[]{:S(2)}) %copy-start) | copy-done | bytes 8216
  0.7 55.7 %cluster_best.1 = f32[1,2048]{1,0:T(1,128)S(1)} custom-call(bf16[2048,1024]{1,0:T(8,128)(2,1)} %emb_hbm.1, s32[1,2048]{1,0:T(1,128)S(1)} %bitcast.3), custom_call_target="tpu_custom_call" | custom-call | tf_op jit(solution)/shard_map/cluster_best/pallas_call | solution.py:328
  56.4 0.6 %copy.4 = f32[2048]{0:T(1024)} copy(f32[2048]{0:T(1024)S(1)} %bitcast.2) | data formatting | bytes 16384
Async XLA Ops:
  0.0 0.7 %copy-start = (s32[2048]{0:T(1024)S(1)}, s32[2048]{0:T(1024)}, u32[]{:S(2)}) copy-start(s32[2048]{0:T(1024)} %param.3) | copy-start | bytes 24580

commit v4 on v3

--- a/solution.py
+++ b/solution.py
@@ -286,18 +286,17 @@
         row = final[PLACE[d] // 2:PLACE[d] // 2 + 1]
         if PLACE[d] % 2:
             row = jnp.concatenate([row[:, SLOTS:], row[:, :SLOTS]], axis=1)
-        ret_out[d] = row
+        ret_out[(y + NY - d) % NY] = row
         if d == 0:
             ret_in[home] = row
-    hops = [(d, e) for d in range(NY) for e in range(NZ) if d or e]
-    hops.sort(key=lambda de: -min(de[0], NY - de[0]) - min(de[1], NZ - de[1]))
-    for d, e in hops:
+    for i in range(NY * NZ - 1):
+        to = i + (i + NY * NZ - home) // (NY * NZ)
         pltpu.make_async_remote_copy(
-            src_ref=ret_out.at[d],
+            src_ref=ret_out.at[to % NY],
             dst_ref=ret_in.at[home],
             send_sem=ret_send,
             recv_sem=ret_recv,
-            device_id=(corpus_id((y + NY - d) % NY, x, k), (z + e) % NZ),
+            device_id=(corpus_id(to % NY, x, k), to // NY),
             device_id_type=MESH,
         ).start()
     returned = whole(ret_in.at[pl.ds(0, NY * NZ - 1)], ret_send, ret_recv)
@@ -349,7 +348,7 @@
             dma, dma, dma, dma,
         ],
         compiler_params=pltpu.CompilerParams(
-            collective_id=0, has_side_effects=True, vmem_limit_bytes=52 * 2 ** 20
+            collective_id=0, has_side_effects=True, vmem_limit_bytes=55222 * 2 ** 10
         ),
         name="cluster_best",
     )(embeddings, cluster_ids.reshape(1, rows))

time: 57.2 us -> 56.1 us (0.981)
  local copies, waits for them, and re-layouts: 1.3 us -> 0.6 us
    unnamed x3 -> x1, local copies, waits for them, and re-layouts: 1.3 us -> 0.6 us
where the time goes in v4:
time: 56.1 us; the launch traced here: 55.9 us
  Pallas kernels  55.3 us (99%)
  local copies, waits for them, and re-layouts  0.6 us (1%)
    pallas_call x1, Pallas kernels, local(): pl.pallas_call(kernel, out_shape=jax.ShapeDtypeStruct((1, rows), jnp.floa...  55.3 us

profile of v4, /device:TPU:1, one launch (start us, length us, event | category | flops | bytes accessed | tf_op | source)
XLA Modules:
  0.0 55.9 jit_solution(9357651601378143313)
XLA Ops:
  0.0 55.3 %cluster_best.1 = f32[1,2048]{1,0:T(1,128)S(1)} custom-call(bf16[2048,1024]{1,0:T(8,128)(2,1)} %emb_hbm.1, s32[1,2048]{1,0:T(1,128)} %bitcast.3), custom_call_target="tpu_custom_call" | custom-call | tf_op jit(solution)/shard_map/cluster_best/pallas_call | solution.py:327
  55.3 0.6 %copy.4 = f32[2048]{0:T(1024)} copy(f32[2048]{0:T(1024)S(1)} %bitcast.2) | data formatting | bytes 16384

commit v5 on v4

--- a/solution.py
+++ b/solution.py
@@ -50,7 +50,7 @@
 
 def kernel(
     emb_hbm, ids_hbm, out_ref,
-    emb, ids_ref, counts, outbox, obuf, lbuf, rbuf, own_t, beside_t, left_t, right_t, part_out, part_in, ret_out, ret_in,
+    emb, ids_ref, counts, thrice, outbox, obuf, lbuf, rbuf, own_t, beside_t, left_t, right_t, part_out, part_in, ret_out, ret_in,
     emb_sem, ids_sem, ysend, yrecv, fsend, frecv, psend, precv,
     ret_send, ret_recv,
 ):
@@ -87,6 +87,8 @@
     clusters = NY * NZ
     member = lax.broadcasted_iota(jnp.int32, (clusters, rows), 0) == ids
     onehot = jnp.where(member, jnp.float32(1.0), jnp.float32(0.0)).astype(jnp.bfloat16)
+    for i in range(3):
+        thrice[i * clusters:(i + 1) * clusters] = onehot
     step = 256
     row_i = lax.broadcasted_iota(jnp.int32, (step, step + LANES), 0)
     col_i = lax.broadcasted_iota(jnp.int32, (step, step + LANES), 1)
@@ -303,13 +305,14 @@
     returned.wait_recv()
 
     table = ret_in[...].reshape(clusters, LANES)[:, :SLOTS]
-    found = jnp.zeros((SLOTS, rows), jnp.float32)
+    terms = []
     for _ in range(3):
-        rounded = table.astype(jnp.bfloat16)
-        table = table - rounded.astype(jnp.float32)
-        found = found + lax.dot_general(
-            rounded, onehot, (((0,), (0,)), ((), ())), preferred_element_type=jnp.float32
-        )
+        terms.append(table.astype(jnp.bfloat16))
+        table = table - terms[-1].astype(jnp.float32)
+    found = lax.dot_general(
+        jnp.concatenate(terms, axis=0), thrice[...], (((0,), (0,)), ((), ())),
+        preferred_element_type=jnp.float32,
+    )
     rank_i = lax.broadcasted_iota(jnp.int32, (SLOTS, rows), 0)
     hit = rank_i == rank.astype(jnp.int32)
     out_ref[...] = jnp.sum(jnp.where(hit, found, 0.0), axis=0, keepdims=True)
@@ -333,6 +336,7 @@
             pltpu.VMEM((rows, width), jnp.bfloat16),
             pltpu.VMEM((1, rows), jnp.int32),
             pltpu.VMEM((NY * NZ, LANES), jnp.float32),
+            pltpu.VMEM((3 * NY * NZ, rows), jnp.bfloat16),
             pltpu.VMEM((NY, SLOTS, width), jnp.bfloat16),
             pltpu.VMEM((2, UNIT, width), jnp.bfloat16),
             pltpu.VMEM((UNIT, width), jnp.bfloat16),

time: 56.1 us -> 56 us (level)
  no operation moved by 1% of the time
where the time goes in v5:
time: 56 us; the launch traced here: 55.8 us
  Pallas kernels  55.2 us (99%)
  local copies, waits for them, and re-layouts  0.6 us (1%)
    pallas_call x1, Pallas kernels, local(): pl.pallas_call(kernel, out_shape=jax.ShapeDtypeStruct((1, rows), jnp.floa...  55.2 us

profile of v5, /device:TPU:1, one launch (start us, length us, event | category | flops | bytes accessed | tf_op | source)
XLA Modules:
  0.0 55.8 jit_solution(14272731234991682220)
XLA Ops:
  0.0 55.2 %cluster_best.1 = f32[1,2048]{1,0:T(1,128)S(1)} custom-call(bf16[2048,1024]{1,0:T(8,128)(2,1)} %emb_hbm.1, s32[1,2048]{1,0:T(1,128)} %bitcast.3), custom_call_target="tpu_custom_call" | custom-call | tf_op jit(solution)/shard_map/cluster_best/pallas_call | solution.py:330
  55.2 0.6 %copy.4 = f32[2048]{0:T(1024)} copy(f32[2048]{0:T(1024)S(1)} %bitcast.2) | data formatting | bytes 16384

commit v6 on v4

--- a/solution.py
+++ b/solution.py
@@ -91,14 +91,16 @@
     row_i = lax.broadcasted_iota(jnp.int32, (step, step + LANES), 0)
     col_i = lax.broadcasted_iota(jnp.int32, (step, step + LANES), 1)
     earlier = ((row_i < col_i) | (col_i >= step)).astype(jnp.bfloat16)
+    parts = [onehot[:, b * step:(b + 1) * step] for b in range(rows // step)]
+    count = jnp.dot(
+        jnp.concatenate(parts, axis=0), earlier, preferred_element_type=jnp.float32
+    ).reshape(len(parts), clusters, step + LANES)
     carry = jnp.zeros((clusters, LANES), jnp.float32)
     ranks = []
-    for b in range(rows // step):
-        part = onehot[:, b * step:(b + 1) * step]
-        count = jnp.dot(part, earlier, preferred_element_type=jnp.float32)
-        before = count[:, :step] + jnp.concatenate([carry] * (step // LANES), axis=1)
+    for b, part in enumerate(parts):
+        before = count[b, :, :step] + jnp.concatenate([carry] * (step // LANES), axis=1)
         ranks.append(jnp.sum(before * part.astype(jnp.float32), axis=0, keepdims=True))
-        carry = carry + count[:, step:]
+        carry = carry + count[b, :, step:]
     rank = jnp.concatenate(ranks, axis=1)
     counts[...] = carry
     key = (ids - z * NY) * SLOTS + rank.astype(jnp.int32)

time: 56.1 us -> 56.1 us (level)
  no operation moved by 1% of the time
where the time goes in v6:
time: 56.1 us; the launch traced here: 55.9 us
  Pallas kernels  55.3 us (99%)
  local copies, waits for them, and re-layouts  0.6 us (1%)
    pallas_call x1, Pallas kernels, local(): pl.pallas_call(kernel, out_shape=jax.ShapeDtypeStruct((1, rows), jnp.floa...  55.3 us

profile of v6, /device:TPU:1, one launch (start us, length us, event | category | flops | bytes accessed | tf_op | source)
XLA Modules:
  0.0 55.9 jit_solution(82255097865787658)
XLA Ops:
  0.0 55.3 %cluster_best.1 = f32[1,2048]{1,0:T(1,128)S(1)} custom-call(bf16[2048,1024]{1,0:T(8,128)(2,1)} %emb_hbm.1, s32[1,2048]{1,0:T(1,128)} %bitcast.3), custom_call_target="tpu_custom_call" | custom-call | tf_op jit(solution)/shard_map/cluster_best/pallas_call | solution.py:329
  55.3 0.6 %copy.4 = f32[2048]{0:T(1024)} copy(f32[2048]{0:T(1024)S(1)} %bitcast.2) | data formatting | bytes 16384
